TPU v7x, 512 devices: a whole 4x4x16 slice. The times are simulated.
512 devices in a mesh: ctx: 64 (over z, y), tp: 8 (over x, core).
Axes of the slice: x: 4, y: 4, z: 16, core: 2. Of those that a mesh axis runs over, the one named last changes fastest.
Arguments:
- queries: bfloat16 [8192, 4096], P('ctx', 'tp'), may hold values from -10 to 10
- stretch_key_value: bfloat16 [2, 8192, 1024], P(None, 'ctx', 'tp'), may hold values from -6 to 6
- cache_kv: bfloat16 [2, 128, 2048, 1024], P(None, None, 'ctx', 'tp'), may hold values from -6 to 6
- chosen: int32 [4, 8, 3], replicated, may hold values from 0 to 127, as said below
- out_weight: bfloat16 [4096, 4096], P('ctx', 'tp'), may hold values from -0.09375 to 0.09375
Outputs:
- attention: bfloat16 [8192, 4096], P('ctx', 'tp')
- mixed: bfloat16 [8192, 4096], P('ctx', 'tp')
Inputs may be any that keep to these rules, and one draw needn't show every extreme that they name: `chosen`: each row names 3 different cache blocks; some row names the first block and the last.
All inputs are finite; a program needn't handle non-finite values.
Results may differ from a plain program's by a relative error of at most 0.0052.
Values may be sent and summed in bfloat16 or wider, within the bound.
A program may use at most 64 MiB of HBM per device.

v0:
```python
import math

import jax
import jax.numpy as jnp
from jax import lax
from jax.sharding import PartitionSpec as P

QUERY_HEAD_COUNT = 32
KEY_VALUE_HEADS = 8
HEAD_SIZE = 128
BLOCK_TOKENS = 2048
CHOSEN_COUNT = 3


def shifted(value, axis, steps):
    count = lax.axis_size(axis)
    leading, last = (max(0, -steps), min(count, count - steps))
    return lax.ppermute(value, axis, [(source, source + steps) for source in range(leading, last)])


def body(queries, stretch_key_value, cache_kv, chosen, out_weight):
    ctx_count = lax.axis_size("ctx")
    ctx_index = lax.axis_index("ctx")
    tp_index = lax.axis_index("tp")
    rows_dev = queries.shape[0]
    kv_heads = cache_kv.shape[3] // HEAD_SIZE
    group_width = QUERY_HEAD_COUNT // KEY_VALUE_HEADS
    block_count = cache_kv.shape[1]
    stripe_len = cache_kv.shape[2]
    stretch_len = rows_dev * ctx_count
    own_len = min(BLOCK_TOKENS, stretch_len)
    score_scale = 1.0 / math.sqrt(HEAD_SIZE)
    my_block = ctx_index * rows_dev // own_len
    my_choices = lax.dynamic_slice_in_dim(chosen, tp_index * kv_heads, kv_heads, 1)
    cache_split = cache_kv.reshape(2, block_count, stripe_len, kv_heads, HEAD_SIZE)
    head_ids = jnp.arange(kv_heads, dtype=jnp.int32)[:, None]
    selected = cache_split[:, my_choices, :, head_ids, :]
    gathered = lax.all_gather(selected, "ctx", axis=4, tiled=True)
    block_kv = lax.dynamic_index_in_dim(gathered, my_block, 0, keepdims=False)
    far_keys = block_kv[:, :, 0].reshape(kv_heads, CHOSEN_COUNT * BLOCK_TOKENS, HEAD_SIZE)
    far_values = block_kv[:, :, 1].reshape(kv_heads, CHOSEN_COUNT * BLOCK_TOKENS, HEAD_SIZE)
    own_block = stretch_key_value
    doubling_steps = (own_len // rows_dev).bit_length() - 1
    for level in range(doubling_steps):
        earlier = shifted(own_block, "ctx", 2**level)
        own_block = jnp.concatenate([earlier, own_block], axis=1)
    window_start = ctx_index * rows_dev + rows_dev - own_len
    own_block = own_block.reshape(2, own_len, kv_heads, HEAD_SIZE)
    query_heads = queries.reshape(rows_dev, kv_heads, group_width, HEAD_SIZE)
    far_scores = (
        jnp.einsum("tgph,gkh->gptk", query_heads, far_keys, preferred_element_type=jnp.float32)
        * score_scale
    )
    near_scores = (
        jnp.einsum("tgph,kgh->gptk", query_heads, own_block[0], preferred_element_type=jnp.float32)
        * score_scale
    )
    query_pos = ctx_index * rows_dev + jnp.arange(rows_dev, dtype=jnp.int32)
    key_pos = window_start + jnp.arange(own_len, dtype=jnp.int32)
    causal_mask = (key_pos[None, :] <= query_pos[:, None]) & (
        key_pos[None, :] >= my_block * own_len
    )
    near_scores = jnp.where(causal_mask[None, None], near_scores, -jnp.inf)
    row_max = jnp.maximum(jnp.max(far_scores, axis=-1), jnp.max(near_scores, axis=-1))
    far_weights = jnp.exp(far_scores - row_max[..., None])
    near_weights = jnp.exp(near_scores - row_max[..., None])
    total_mass = jnp.sum(far_weights, axis=-1) + jnp.sum(near_weights, axis=-1)
    far_rounded = far_weights.astype(jnp.bfloat16)
    near_rounded = near_weights.astype(jnp.bfloat16)
    weighted = jnp.einsum(
        "gptk,gkh->tgph", far_rounded, far_values, preferred_element_type=jnp.float32
    )
    weighted = weighted + jnp.einsum(
        "gptk,kgh->tgph", near_rounded, own_block[1], preferred_element_type=jnp.float32
    )
    result = weighted / jnp.transpose(total_mass, (2, 0, 1))[..., None]
    attention = result.astype(jnp.bfloat16).reshape(rows_dev, kv_heads * group_width * HEAD_SIZE)
    heads_all = lax.all_gather(attention, "tp", axis=1, tiled=True)
    projected = jnp.dot(
        heads_all,
        lax.all_gather(out_weight, "ctx", axis=0, tiled=True),
        preferred_element_type=jnp.float32,
    )
    return (attention, projected.astype(jnp.bfloat16))


def solution(mesh):
    in_specs = (
        P("ctx", "tp"),
        P(None, "ctx", "tp"),
        P(None, None, "ctx", "tp"),
        P(),
        P("ctx", "tp"),
    )
    out_specs = (P("ctx", "tp"), P("ctx", "tp"))
    return jax.shard_map(body, mesh=mesh, in_specs=in_specs, out_specs=out_specs, check_vma=False)
```

profile of v0, /device:TPU:1, one launch (start us, length us, event | category | flops | bytes accessed | tf_op | source)
XLA Modules:
  0.0 408.2 jit_solution(16122210849574728306)
XLA Ops:
  7.2 1.0 fusion.29
  8.3 0.1 copy.27
  8.5 0.3 copy-done
  8.8 1.3 gather_fusion
  10.1 0.7 all-gather.7.cloned.1.call-update
  10.9 4.0 collective-permute-start
  14.9 1.6 collective-permute-done
  16.6 0.9 pad_maximum_fusion.2
  17.4 5.2 %collective-permute-start.1 = (bf16[2,256,128]{2,1,0:T(8,128)(2,1)S(1)}, bf16[2,256,128]{2,1,0:T(8,128)(2,1)S(1)}, u32[]{:S(2)}, u32[]{:S(2)}) collective-permute-start(bf16[2,256,128]{2,1,0:T(8,128)(2,1)S(1)} %pad_maximum_fusion.2), channel_id=1, source_target_pairs={{0,16},{8,24},{16,32},{24,40},{32,48},{40,56},{48,64},{56,72},{64,... | collective-permute-start | bytes 393224 | tf_op jit(solution)/shard_map/ppermute | solution.py:18
  22.6 1.9 collective-permute-done.1
  24.6 0.9 pad_maximum_fusion.1
  25.4 7.0 %collective-permute-start.2 = (bf16[2,512,128]{2,1,0:T(8,128)(2,1)S(1)}, bf16[2,512,128]{2,1,0:T(8,128)(2,1)S(1)}, u32[]{:S(2)}, u32[]{:S(2)}) collective-permute-start(bf16[2,512,128]{2,1,0:T(8,128)(2,1)S(1)} %pad_maximum_fusion.1), channel_id=1, source_target_pairs={{0,32},{8,40},{16,48},{24,56},{32,64},{40,72},{48,80},{56,88},{64,... | collective-permute-start | bytes 786440 | tf_op jit(solution)/shard_map/ppermute | solution.py:18
  32.5 4.6 %collective-permute-done.2 = bf16[2,512,128]{2,1,0:T(8,128)(2,1)S(1)} collective-permute-done((bf16[2,512,128]{2,1,0:T(8,128)(2,1)S(1)}, bf16[2,512,128]{2,1,0:T(8,128)(2,1)S(1)}, u32[]{:S(2)}, u32[]{:S(2)}) %collective-permute-start.2) | collective-permute-done | bytes 262176 | tf_op jit(solution)/shard_map/ppermute | solution.py:18
  37.2 0.9 pad_maximum_fusion
  38.0 5.5 %collective-permute-start.3 = (bf16[2,1024,128]{2,1,0:T(8,128)(2,1)S(1)}, bf16[2,1024,128]{2,1,0:T(8,128)(2,1)S(1)}, u32[]{:S(2)}, u32[]{:S(2)}) collective-permute-start(bf16[2,1024,128]{2,1,0:T(8,128)(2,1)S(1)} %pad_maximum_fusion), channel_id=1, source_target_pairs={{0,64},{8,72},{16,80},{24,88},{32,96},{40,104},{48,112},{56,120},{... | collective-permute-start | bytes 1572872 | tf_op jit(solution)/shard_map/ppermute | solution.py:18
  43.5 1.5 compare_and_fusion
  45.0 10.1 %collective-permute-done.3 = bf16[2,1024,128]{2,1,0:T(8,128)(2,1)S(1)} collective-permute-done((bf16[2,1024,128]{2,1,0:T(8,128)(2,1)S(1)}, bf16[2,1024,128]{2,1,0:T(8,128)(2,1)S(1)}, u32[]{:S(2)}, u32[]{:S(2)}) %collective-permute-start.3) | collective-permute-done | bytes 524320 | tf_op jit(solution)/shard_map/ppermute | solution.py:18
  55.3 0.9 constant_dynamic-update-slice_fusion.1
  56.1 0.9 constant_dynamic-update-slice_fusion
  57.0 3.6 fusion.34
  60.5 156.5 %all-gather.9.cloned.1.call-done = bf16[4,3,2,2048,128]{4,3,2,1,0:T(8,128)(2,1)} async-done(((bf16[4,3,2,32,128]{4,3,2,1,0:T(8,128)(2,1)}), bf16[4,3,2,2048,128]{4,3,2,1,0:T(8,128)(2,1)}) %all-gather.9.cloned.1.call-update) | async-done | bytes 12582928 | tf_op jit(solution)/shard_map/all_gather | solution.py:38
  217.1 2.1 constant_dynamic-slice_fusion
  219.2 1.8 bitcast_reduce_fusion
  221.0 0.4 copy-done.1
  221.4 0.6 fusion.6
  221.9 2.0 fusion.1
  224.0 2.2 fusion.4
  226.2 1.5 fusion.21
  227.8 1.7 copy.34
  229.4 131.3 %all-gather.7.cloned.1.call-done = bf16[4096,512]{1,0:T(8,128)(2,1)} async-done(((bf16[64,512]{1,0:T(8,128)(2,1)}), bf16[4096,512]{1,0:T(8,128)(2,1)}) %all-gather.7.cloned.1.call-update) | async-done | bytes 4194320 | tf_op jit(solution)/shard_map/all_gather | solution.py:81
  360.7 37.1 %all-gather.5.cloned.1.call-done = bf16[128,4096]{0,1:T(8,128)(2,1)} async-done(((bf16[128,512]{0,1:T(8,128)(2,1)}), bf16[128,4096]{0,1:T(8,128)(2,1)}) %all-gather.5.cloned.1.call-update) | async-done | bytes 1048592 | tf_op jit(solution)/shard_map/all_gather | solution.py:78
  397.8 3.9 convolution_convert_fusion
  (25 shorter events, 0.4 us)
Async XLA Ops:
  7.2 1.6 copy-start
  7.2 209.9 %all-gather.9.cloned.1.call-start = ((), (), s32[]{:S(2)}) async-start(), calls=%async_computation.2 | async-start | bytes 12779520 | tf_op jit(solution)/shard_map/all_gather | solution.py:38
  10.1 350.6 %all-gather.7.cloned.1.call-start = ((), (), s32[]{:S(2)}) async-start(), calls=%async_computation.1 | async-start | bytes 4259840 | tf_op jit(solution)/shard_map/all_gather | solution.py:81
  10.8 387.0 %all-gather.5.cloned.1.call-start = ((), (), s32[]{:S(2)}) async-start(), calls=%async_computation | async-start | bytes 1179648 | tf_op jit(solution)/shard_map/all_gather | solution.py:78
  10.9 5.7 %collective-permute-start = (bf16[2,128,128]{2,1,0:T(8,128)(2,1)}, bf16[2,128,128]{2,1,0:T(8,128)(2,1)S(1)}, u32[]{:S(2)}, u32[]{:S(2)}) collective-permute-start(bf16[2,128,128]{2,1,0:T(8,128)(2,1)} %param.6), channel_id=1, source_target_pairs={{0,8},{8,16},{16,24},{24,32},{32,40},{40,48},{48,56},{56,64},{64,7... | collective-permute-start | bytes 196616 | tf_op jit(solution)/shard_map/ppermute | solution.py:18
  16.6 28.5 %copy-start.3 = (bf16[2,128,128]{2,1,0:T(8,128)(2,1)}, bf16[2,128,128]{2,1,0:T(8,128)(2,1)S(1)}, u32[]{:S(2)}) copy-start(bf16[2,128,128]{2,1,0:T(8,128)(2,1)S(1)} %collective-permute-done) | copy-start | bytes 196612
  17.4 7.1 %collective-permute-start.1 = (bf16[2,256,128]{2,1,0:T(8,128)(2,1)S(1)}, bf16[2,256,128]{2,1,0:T(8,128)(2,1)S(1)}, u32[]{:S(2)}, u32[]{:S(2)}) collective-permute-start(bf16[2,256,128]{2,1,0:T(8,128)(2,1)S(1)} %pad_maximum_fusion.2), channel_id=1, source_target_pairs={{0,16},{8,24},{16,32},{24,40},{32,48},{40,56},{48,64},{56,72},{64,... | collective-permute-start | bytes 393224 | tf_op jit(solution)/shard_map/ppermute | solution.py:18
  25.4 11.7 %collective-permute-start.2 = (bf16[2,512,128]{2,1,0:T(8,128)(2,1)S(1)}, bf16[2,512,128]{2,1,0:T(8,128)(2,1)S(1)}, u32[]{:S(2)}, u32[]{:S(2)}) collective-permute-start(bf16[2,512,128]{2,1,0:T(8,128)(2,1)S(1)} %pad_maximum_fusion.1), channel_id=1, source_target_pairs={{0,32},{8,40},{16,48},{24,56},{32,64},{40,72},{48,80},{56,88},{64,... | collective-permute-start | bytes 786440 | tf_op jit(solution)/shard_map/ppermute | solution.py:18
  38.0 17.1 %collective-permute-start.3 = (bf16[2,1024,128]{2,1,0:T(8,128)(2,1)S(1)}, bf16[2,1024,128]{2,1,0:T(8,128)(2,1)S(1)}, u32[]{:S(2)}, u32[]{:S(2)}) collective-permute-start(bf16[2,1024,128]{2,1,0:T(8,128)(2,1)S(1)} %pad_maximum_fusion), channel_id=1, source_target_pairs={{0,64},{8,72},{16,80},{24,88},{32,96},{40,104},{48,112},{56,120},{... | collective-permute-start | bytes 1572872 | tf_op jit(solution)/shard_map/ppermute | solution.py:18
  60.5 158.6 %copy-start.4 = (bf16[128,512]{1,0:T(8,128)(2,1)S(1)}, bf16[128,512]{1,0:T(8,128)(2,1)}, u32[]{:S(2)}) copy-start(bf16[128,512]{1,0:T(8,128)(2,1)} %param.5) | copy-start | bytes 393220
  219.2 2.2 copy-start.1
  224.0 2.2 copy-start.2
Sparse Core Ops, SparseCore 0:
  10.9 206.0 all-gather.8
  220.0 140.6 all-gather.6
  363.4 34.2 all-gather.4
where the time goes:
time: 409 us; the launch traced here: 408 us
  waiting for transfers between devices  344 us (84%)
  starting transfers between devices  21.9 us (5%)
  between operations  14 us (3%)
  matrix products  13 us (3%)
  other arithmetic  7.78 us (2%)
  local copies, waits for them, and re-layouts  7.69 us (2%)
    all_gather x1, waiting for transfers between devices, body(): gathered = lax.all_gather(selected, 'ctx', axis=4, tiled=True)  157 us
    all_gather x1, waiting for transfers between devices, body(): lax.all_gather(out_weight, 'ctx', axis=0, tiled=True)  131 us
    all_gather x1, waiting for transfers between devices, body(): heads_all = lax.all_gather(attention, 'tp', axis=1, tiled=True)  37.1 us
    ppermute x4, starting transfers between devices, shifted(): lax.ppermute(value, axis, [(source, source + steps) for source in range(l...  21.8 us
    ppermute x4, waiting for transfers between devices, shifted(): lax.ppermute(value, axis, [(source, source + steps) for source in range(l...  18.3 us
  transfers between devices with their start and end apart: 7, of which 7 were waited for; matrix products, arithmetic and copies ran while one was open for 5% of the time, Pallas kernels for 0%

commit v1 on v0

v1 whole, which is shorter than its diff:
```python
import math

import jax
import jax.numpy as jnp
from jax import lax
from jax.experimental import pallas as pl
from jax.experimental.pallas import tpu as pltpu
from jax.sharding import PartitionSpec as P

MESH = pl.DeviceIdType.MESH
HEAD = 128
HEADS = 4
SCALE_LOG2 = math.log2(math.e) / math.sqrt(HEAD)
PIECE = 96
NEAR, OWN, CHAIN = 0, 512, 896
BF16, F32 = jnp.bfloat16, jnp.float32


def kernel(
    q_ref, skv_ref, cache_ref, chosen_ref, w_ref, att_ref, mix_ref,
    kvsend, kv, qbuf, acc, mst, lst, obuf, ost, orecv, ostr, abuf, wbuf, res, resrecv,
    s_far, s_own, s_near, s_chain, s_q, s_o, s_st, s_a, s_w0, s_wp, s_wm, s_ws, s_out,
    r_own, r_near, r_chain, r_q, r_o, r_st, r_a, r_w0, r_wp, r_wm, r_ws, r_out,
):
    ctx, tp = lax.axis_index("ctx"), lax.axis_index("tp")
    z, y, x, c = ctx // 4, ctx % 4, tp // 2, tp % 2
    qz, zq = z // 4, z % 4
    py = y % 2
    ypair = y + 1 - 2 * py
    same = c == py

    def dev(zz, yy, xx, cc):
        return (zz * 4 + yy, xx * 2 + cc)

    def rcopy(src, dst, ssem, rsem, to):
        return pltpu.make_async_remote_copy(
            src_ref=src, dst_ref=dst, send_sem=ssem, recv_sem=rsem, device_id=to, device_id_type=MESH
        )

    me = dev(z, y, x, c)

    barrier = pltpu.get_barrier_semaphore()

    def greet(to):
        pl.semaphore_signal(barrier, inc=1, device_id=to, device_id_type=MESH)

    for d in range(1, 4):
        greet(dev(4 * qz + (zq + d) % 4, y, x, c))
        greet(dev(z, (y + d) % 4, x, c))
    greet(dev((z + 1) % 16, y, x, c))
    greet(dev((z + 15) % 16, y, x, c))
    greet(dev(z, y, x, 1 - c))

    @pl.when(zq == 0)
    def _():
        for k in range(4):
            greet(dev(4 * ((qz + 3) % 4) + k, y, x, c))
        for k in (2, 3):
            greet(dev(4 * ((qz + 2) % 4) + k, y, x, c))

    @pl.when(zq == 3)
    def _():
        for k in range(4):
            greet(dev(4 * ((qz + 1) % 4) + k, y, x, c))
        for k in (0, 1):
            greet(dev(4 * ((qz + 2) % 4) + k, y, x, c))

    mine = y - py + c
    for d in range(4):
        yy = (y + d) % 4
        if d == 0:
            @pl.when(jnp.logical_not(same))
            def _():
                greet(dev(z, yy, x, py))
        else:
            greet(dev(z, yy, x, py))
        xx = (x + d) % 4
        for k in range(2):
            if d == 0:
                @pl.when(jnp.logical_not(jnp.logical_and(same, k == c)))
                def _():
                    greet(dev(z, mine, xx, k))
            else:
                greet(dev(z, mine, xx, k))
    pl.semaphore_wait(barrier, 24 - 2 * same.astype(jnp.int32))

    for b in range(4):
        for j in range(3):
            idx = chosen_ref[b, tp, j]
            kvsend[b, 0, 32 * j : 32 * j + 32] = cache_ref[0, idx]
            kvsend[b, 1, 32 * j : 32 * j + 32] = cache_ref[1, idx]

    def kvrows(first, count=PIECE):
        return kv.at[:, pl.ds(pl.multiple_of(first, 32), count), :]

    up = zq // 2
    far = [
        ((qz + 1) % 4, 0, 3 - zq),
        ((qz + 3) % 4, 3, 6 + zq),
        ((qz + 2) % 4, 3 * (1 - up), up * (7 - zq) + (1 - up) * (10 + zq)),
    ]
    far = [
        rcopy(kvsend.at[b], kvrows(CHAIN + PIECE * i), s_far.at[n], r_chain.at[i], dev(4 * b + e, y, x, c))
        for n, (b, e, i) in enumerate(far)
    ]
    for n in (2, 0, 1):
        far[n].start()
    qs = [
        rcopy(q_ref, qbuf.at[y], s_q.at[d - 1], r_q.at[d - 1], dev(z, (y + d) % 4, x, c)) for d in (1, 2, 3)
    ]
    for cp in qs:
        cp.start()
    own = [
        rcopy(
            kvsend.at[qz], kvrows(OWN + PIECE * zq), s_own.at[d - 1], r_own.at[d - 1],
            dev(4 * qz + (zq + d) % 4, y, x, c),
        )
        for d in (1, 2, 3)
    ]
    for cp in own:
        cp.start()
    near = [
        rcopy(
            skv_ref, kvrows(NEAR + 128 * zq, 128), s_near.at[d - 1], r_near.at[d - 1],
            dev(4 * qz + (zq + d) % 4, y, x, c),
        )
        for d in (1, 2, 3)
    ]
    for d in (1, 2, 3):
        pl.when(zq + d < 4)(near[d - 1].start)
    w0 = []
    for t in range(2):
        for k in range(2):
            yy = c + 2 * t
            cp = rcopy(w_ref, wbuf.at[ctx], s_w0.at[2 * t + k], r_w0.at[y], dev(z, yy, x, k))
            notself = jnp.logical_not(jnp.logical_and(yy == y, k == c))
            pl.when(notself)(cp.start)
            w0.append((cp, notself))

    qbuf[y] = q_ref[...]
    kv[:, pl.ds(pl.multiple_of(OWN + PIECE * zq, 32), PIECE), :] = kvsend[qz]
    for k in range(4):
        @pl.when(k == zq)
        def _():
            kv[:, 128 * k : 128 * k + 128, :] = skv_ref[...]

        @pl.when(k > zq)
        def _():
            kv[:, 128 * k : 128 * k + 128, :] = jnp.zeros((2, 128, HEAD), BF16)

    @pl.when(same)
    def _():
        wbuf[ctx] = w_ref[...]

    mst[...] = jnp.full(mst.shape, -1e30, F32)
    lst[...] = jnp.zeros(lst.shape, F32)
    acc[...] = jnp.zeros(acc.shape, F32)

    def chain(i):
        for idx, ok, to in ((i, zq < 3, z + 1), (6 + i, zq > 0, z - 1)):
            rows = kvrows(CHAIN + PIECE * idx)
            cp = rcopy(rows, rows, s_chain.at[idx], r_chain.at[idx], dev(to, y, x, c))
            cp.wait_recv()
            pl.when(ok)(cp.start)

    def chain_sent(i):
        for idx, ok, to in ((i, zq < 3, z + 1), (6 + i, zq > 0, z - 1)):
            rows = kvrows(CHAIN + PIECE * idx)
            cp = rcopy(rows, rows, s_chain.at[idx], r_chain.at[idx], dev(to, y, x, c))
            pl.when(ok)(cp.wait_send)

    def wblock(origin):
        return wbuf.at[pl.ds(4 * ((origin + 32) % 16) + 2 * c, 2)]

    def wcopies(t):
        up_block, down_block = wblock(z - (t - 1)), wblock(z + (t - 1))
        ups = rcopy(up_block, up_block, s_wp.at[t - 1], r_wp.at[t - 1], dev((z + 1) % 16, y, x, c))
        downs = None
        if t <= 7:
            downs = rcopy(down_block, down_block, s_wm.at[t - 1], r_wm.at[t - 1], dev((z + 15) % 16, y, x, c))
        return ups, downs

    def wsibling(t):
        sib = dev(z, y, x, 1 - c)
        ub, db = wblock(z - t), wblock(z + t)
        out = [rcopy(ub, ub, s_ws.at[t - 1], r_ws.at[t - 1], sib)]
        if t <= 7:
            out.append(rcopy(db, db, s_ws.at[7 + t], r_ws.at[7 + t], sib))
        return out

    def wstart(t):
        for cp in wcopies(t):
            if cp is not None:
                cp.start()

    def wstep(t):
        for cp in wcopies(t):
            if cp is not None:
                cp.wait_recv()
        if t < 8:
            wstart(t + 1)
        for cp in wsibling(t):
            cp.start()

    def attend(first, count, masked):
        def one(h, _):
            qh = qbuf[:, :, pl.ds(pl.multiple_of(h * HEAD, HEAD), HEAD)].reshape(512, HEAD)
            s = lax.dot_general(
                kv[0, first : first + count], qh, (((1,), (1,)), ((), ())), preferred_element_type=F32
            )
            if masked:
                key = lax.broadcasted_iota(jnp.int32, (count, 512), 0)
                row = lax.broadcasted_iota(jnp.int32, (count, 512), 1)
                pos = (key // 128) * 512 + y * 128 + key % 128
                s = jnp.where(pos <= row + 512 * zq, s, -jnp.inf)
            before = mst[h]
            top = jnp.maximum(before, jnp.max(s, axis=0, keepdims=True))
            p = jnp.exp2((s - top) * SCALE_LOG2)
            shrink = jnp.exp2((before - top) * SCALE_LOG2)
            mst[h] = top
            lst[h] = lst[h] * shrink + jnp.sum(p, axis=0, keepdims=True)
            acc[h] = acc[h] * shrink + lax.dot_general(
                kv[1, first : first + count], p.astype(BF16), (((0,), (0,)), ((), ())),
                preferred_element_type=F32,
            )
            return 0

        lax.fori_loop(0, HEADS, one, 0)

    for cp in qs:
        cp.wait_recv()
    for i in range(6):
        chain(i)
    for cp, ns in w0:
        pass
    for k in range(4):
        cp = rcopy(w_ref, wbuf.at[4 * z + k], s_w0.at[0], r_w0.at[k], me)
        pl.when(jnp.logical_not(jnp.logical_and(same, k == y)))(cp.wait_recv)
    wstart(1)
    for cp in own:
        cp.wait_recv()
    attend(OWN, 384, False)
    wstep(1)
    for d in (1, 2, 3):
        pl.when(zq >= d)(near[d - 1].wait_recv)
    attend(NEAR, 512, True)
    wstep(2)
    attend(CHAIN, 576, False)
    wstep(3)
    attend(CHAIN + 576, 576, False)

    def finish(h, _):
        o = acc[h] * (1.0 / lst[h])
        for r in range(4):
            obuf[r, h] = o[:, r * 128 : r * 128 + 128].astype(BF16)
            ost[r, h] = mst[h][:, r * 128 : r * 128 + 128]
            ost[r, HEADS + h] = lst[h][:, r * 128 : r * 128 + 128]
        return 0

    lax.fori_loop(0, HEADS, finish, 0)
    ocp, scp = [], []
    for d in (1, 2, 3):
        r = (y + d) % 4
        ocp.append(rcopy(obuf.at[r], orecv.at[d - 1], s_o.at[d - 1], r_o.at[d - 1], dev(z, r, x, c)))
        scp.append(rcopy(ost.at[r], ostr.at[d - 1], s_st.at[d - 1], r_st.at[d - 1], dev(z, r, x, c)))
    for n in (1, 0, 2):
        scp[n].start()
        ocp[n].start()
    wstep(4)
    for n in range(3):
        scp[n].wait_recv()
        ocp[n].wait_recv()

    for h in range(HEADS):
        ms = [ost[y, h]] + [ostr[n, h] for n in range(3)]
        ls = [ost[y, HEADS + h]] + [ostr[n, HEADS + h] for n in range(3)]
        os_ = [obuf[y, h]] + [orecv[n, h] for n in range(3)]
        top = jnp.maximum(jnp.maximum(ms[0], ms[1]), jnp.maximum(ms[2], ms[3]))
        ws = [l * jnp.exp2((m - top) * SCALE_LOG2) for m, l in zip(ms, ls)]
        inv = 1.0 / (ws[0] + ws[1] + ws[2] + ws[3])
        o = sum(o_.astype(F32) * (w * inv) for o_, w in zip(os_, ws))
        att_ref[:, h * HEAD : h * HEAD + HEAD] = o.T.astype(BF16)

    acp = []
    for d in (2, 1, 3, 0):
        xx = (x + d) % 4
        for t in range(2):
            yy = ypair if t == 0 else y
            cp = rcopy(att_ref, abuf.at[tp], s_a.at[2 * d + t], r_a.at[tp], dev(z, yy, xx, py))
            if d == 0 and t == 1:
                pl.when(jnp.logical_not(same))(cp.start)
            else:
                cp.start()
            acp.append((cp, d == 0 and t == 1))

    @pl.when(same)
    def _():
        abuf[tp] = att_ref[...]

    for t in (5, 6, 7, 8):
        wstep(t)
    for g in range(8):
        cp = rcopy(att_ref, abuf.at[g], s_a.at[0], r_a.at[g], me)
        pl.when(jnp.logical_not(jnp.logical_and(same, tp == g)))(cp.wait_recv)
    for t in range(1, 9):
        for n, cp in enumerate(wsibling(t)):
            ob = 4 * ((z - t + 32) % 16 if n == 0 else (z + t) % 16) + 2 * (1 - c)
            blk = wbuf.at[pl.ds(ob, 2)]
            rcopy(blk, blk, s_ws.at[0], r_ws.at[t - 1 if n == 0 else 7 + t], me).wait_recv()

    def project(g, total):
        return total + jnp.dot(abuf[g], wbuf[pl.ds(8 * g, 8)].reshape(512, 512), preferred_element_type=F32)

    res[...] = lax.fori_loop(0, 8, project, jnp.zeros((128, 512), F32)).astype(BF16)
    out = rcopy(res, resrecv, s_out.at[0], r_out.at[0], dev(z, ypair, x, 1 - c))

    @pl.when(same)
    def _():
        mix_ref[...] = res[...]

    @pl.when(jnp.logical_not(same))
    def _():
        out.start()
        out.wait()
        mix_ref[...] = resrecv[...]

    for cp in far + qs + own + ocp + scp:
        cp.wait_send()
    for d in (1, 2, 3):
        pl.when(zq + d < 4)(near[d - 1].wait_send)
    for cp, ns in w0:
        pl.when(ns)(cp.wait_send)
    for i in range(6):
        chain_sent(i)
    for cp, maybe in acp:
        if maybe:
            pl.when(jnp.logical_not(same))(cp.wait_send)
        else:
            cp.wait_send()
    for t in range(1, 9):
        for cp in wcopies(t):
            if cp is not None:
                cp.wait_send()
        for cp in wsibling(t):
            cp.wait_send()


def body(queries, stretch_key_value, cache_kv, chosen, out_weight):
    dma = lambda n: pltpu.SemaphoreType.DMA((n,))
    vmem = pl.BlockSpec(memory_space=pltpu.VMEM)
    return pl.pallas_call(
        kernel,
        out_shape=(jax.ShapeDtypeStruct((128, 512), BF16), jax.ShapeDtypeStruct((128, 512), BF16)),
        in_specs=[vmem, vmem, vmem, pl.BlockSpec(memory_space=pltpu.SMEM), vmem],
        out_specs=(vmem, vmem),
        scratch_shapes=[
            pltpu.VMEM((4, 2, PIECE, HEAD), BF16),
            pltpu.VMEM((2, 2048, HEAD), BF16),
            pltpu.VMEM((4, 128, 512), BF16),
            pltpu.VMEM((HEADS, HEAD, 512), F32),
            pltpu.VMEM((HEADS, 1, 512), F32),
            pltpu.VMEM((HEADS, 1, 512), F32),
            pltpu.VMEM((4, HEADS, HEAD, 128), BF16),
            pltpu.VMEM((4, 2 * HEADS, 1, 128), F32),
            pltpu.VMEM((3, HEADS, HEAD, 128), BF16),
            pltpu.VMEM((3, 2 * HEADS, 1, 128), F32),
            pltpu.VMEM((8, 128, 512), BF16),
            pltpu.VMEM((64, 64, 512), BF16),
            pltpu.VMEM((128, 512), BF16),
            pltpu.VMEM((128, 512), BF16),
        ]
        + [dma(n) for n in (3, 3, 3, 12, 3, 3, 3, 8, 4, 8, 7, 15, 1)]
        + [dma(n) for n in (3, 3, 12, 3, 3, 3, 8, 4, 8, 7, 15, 1)],
        compiler_params=pltpu.CompilerParams(
            collective_id=0, has_side_effects=True, vmem_limit_bytes=56 * 2**20
        ),
        cost_estimate=pl.CostEstimate(flops=2 * 2**30, bytes_accessed=4 * 2**20, transcendentals=2**22),
    )(queries, stretch_key_value, cache_kv, chosen, out_weight)


def solution(mesh):
    in_specs = (
        P("ctx", "tp"),
        P(None, "ctx", "tp"),
        P(None, None, "ctx", "tp"),
        P(),
        P("ctx", "tp"),
    )
    out_specs = (P("ctx", "tp"), P("ctx", "tp"))
    return jax.shard_map(body, mesh=mesh, in_specs=in_specs, out_specs=out_specs, check_vma=False)
```

time: 409 us -> 190 us (0.46)
  waiting for transfers between devices: 344 us -> 0 us
  Pallas kernels: 0 us -> 185 us
  starting transfers between devices: 21.9 us -> 0 us
  between operations: 14 us -> 0.64 us
  matrix products: 13 us -> 0 us
  other arithmetic: 7.78 us -> 0 us
    all_gather x3 -> x0, waiting for transfers between devices: 325 us -> none  [the longest x1 157 us: body(): gathered = lax.all_gather(selected, 'ctx', axis=4, tiled=True)]
    pallas_call x0 -> x1, Pallas kernels: none -> 185 us  [body(): pl.pallas_call(kernel, out_shape=(jax.ShapeDtypeStruct((128, 512), BF16),...]
    ppermute x4 -> x0, starting transfers between devices: 21.8 us -> none  [shifted(): lax.ppermute(value, axis, [(source, source + steps) for source in range(l...]
    ppermute x4 -> x0, waiting for transfers between devices: 18.3 us -> none  [shifted(): lax.ppermute(value, axis, [(source, source + steps) for source in range(l...]
    dot_general x5 -> x0, matrix products: 13 us -> none  [the longest x1 3.92 us: body(): jnp.dot(heads_all, lax.all_gather(out_weight, 'ctx', axis=0, tiled=True),...]
  transfers between devices with their start and end apart: 7 -> 0, of which waited for: 7 -> 0; matrix products, arithmetic and copies ran while one was open for 5% -> 0% of each run, Pallas kernels for 0% -> 0%
where the time goes in v1:
time: 190 us
  Pallas kernels  185 us (97%)
  local copies, waits for them, and re-layouts  4.52 us (2%)
    pallas_call x1, Pallas kernels, body(): pl.pallas_call(kernel, out_shape=(jax.ShapeDtypeStruct((128, 512), BF16),...  185 us
    unnamed x3, local copies, waits for them, and re-layouts  4.52 us

profile of v1, /device:TPU:1, one launch (start us, length us, event | category | flops | bytes accessed | tf_op | source)
XLA Modules:
  0.0 189.9 jit_solution(9637278481346413378)
XLA Ops:
  0.6 1.4 copy.7.chosen_ref
  2.0 184.8 %shard_map.68 = (bf16[128,512]{1,0:T(8,128)(2,1)}, bf16[128,512]{1,0:T(8,128)(2,1)}) custom-call(bf16[128,512]{1,0:T(8,128)(2,1)} %q_ref.1, bf16[2,128,128]{2,1,0:T(8,128)(2,1)} %skv_ref.1, bf16[2,128,32,128]{3,2,1,0:T(8,128)(2,1)} %cache_ref.1, s32[4,8,3]{2,1,0:T(8,128)} %copy.7.chosen_ref, bf16[64,512]{1,0:T(8,128)(2,1)} %w_ref.1), custom_call_target="tpu_custom_call" | custom-call | flops 2147483648 | bytes 4194304 | tf_op jit(solution)/shard_map/pallas_call | solution.py:351
  186.8 1.6 copy.10
  188.4 1.6 copy.11

commit v2 on v1

v2 whole, which is shorter than its diff:
```python
import math

import jax
import jax.numpy as jnp
from jax import lax
from jax.experimental import pallas as pl
from jax.experimental.pallas import tpu as pltpu
from jax.sharding import PartitionSpec as P

MESH = pl.DeviceIdType.MESH
HEAD = 128
HEADS = 4
SCALE_LOG2 = math.log2(math.e) / math.sqrt(HEAD)
PIECE = 96
NEAR, OWN, CHAIN = 0, 512, 896
PARTS = 2
SLOTS = ((0,"w"),(0,""),(0,""),(0,""),(0,"q o O"),(0,"r n"),(0,"N"),(1,""),(0,"A"),(1,""),(0,"C"),(1,""),(0,"B"),(1,""),(0,""),(1,"D"))
LAG = 3
MID, LATE = (1,3), (3,3)
BF16, F32 = jnp.bfloat16, jnp.float32


def kernel(
    q_ref, skv_ref, cache_ref, chosen_ref, w_ref, att_ref, mix_ref,
    kvsend, kv, qsend, qbuf, acc, mst, lst, obuf, ost, orecv, ostr, abuf, abuf_out, wbuf, res, resrecv,
    s_far, s_own, s_near, s_chain, s_q, s_o, s_st, s_a, s_w0, s_w, s_out,
    r_own, r_near, r_chain, r_q, r_o, r_st, r_a, r_w0, r_wp, r_wm, r_ws, r_out,
):
    ctx, tp = lax.axis_index("ctx"), lax.axis_index("tp")
    z, y, x, c = ctx // 4, ctx % 4, tp // 2, tp % 2
    qz, zq = z // 4, z % 4
    py = y % 2
    ypair = y + 1 - 2 * py
    same = c == py

    def dev(zz, yy, xx, cc):
        return (zz * 4 + yy, xx * 2 + cc)

    def rcopy(src, dst, ssem, rsem, to):
        return pltpu.make_async_remote_copy(
            src_ref=src, dst_ref=dst, send_sem=ssem, recv_sem=rsem, device_id=to, device_id_type=MESH
        )

    me = dev(z, y, x, c)

    barrier = pltpu.get_barrier_semaphore()

    def greet(to):
        pl.semaphore_signal(barrier, inc=1, device_id=to, device_id_type=MESH)

    for d in range(1, 4):
        greet(dev(4 * qz + (zq + d) % 4, y, x, c))
        greet(dev(z, (y + d) % 4, x, c))
    greet(dev((z + 1) % 16, y, x, c))
    greet(dev((z + 15) % 16, y, x, c))
    greet(dev(z, y, x, 1 - c))

    @pl.when(zq == 0)
    def _():
        for k in range(4):
            greet(dev(4 * ((qz + 3) % 4) + k, y, x, c))
        for k in (2, 3):
            greet(dev(4 * ((qz + 2) % 4) + k, y, x, c))

    @pl.when(zq == 3)
    def _():
        for k in range(4):
            greet(dev(4 * ((qz + 1) % 4) + k, y, x, c))
        for k in (0, 1):
            greet(dev(4 * ((qz + 2) % 4) + k, y, x, c))

    mine = y - py + c
    for d in range(4):
        yy = (y + d) % 4
        if d == 0:
            @pl.when(jnp.logical_not(same))
            def _():
                greet(dev(z, yy, x, py))
        else:
            greet(dev(z, yy, x, py))
        xx = (x + d) % 4
        for k in range(2):
            if d == 0:
                @pl.when(jnp.logical_not(jnp.logical_and(same, k == c)))
                def _():
                    greet(dev(z, mine, xx, k))
            else:
                greet(dev(z, mine, xx, k))
    pl.semaphore_wait(barrier, 24 - 2 * same.astype(jnp.int32))

    for b in range(4):
        for j in range(3):
            idx = chosen_ref[j, b, tp]
            kvsend[b, 0, 32 * j : 32 * j + 32] = cache_ref[0, idx]
            kvsend[b, 1, 32 * j : 32 * j + 32] = cache_ref[1, idx]

    def kvrows(first, count=PIECE):
        return kv.at[:, pl.ds(pl.multiple_of(first, 32), count), :]

    up = zq // 2
    far = [
        ((qz + 1) % 4, 0, 3 - zq),
        ((qz + 3) % 4, 3, 6 + zq),
        ((qz + 2) % 4, 3 * (1 - up), up * (7 - zq) + (1 - up) * (10 + zq)),
    ]
    far = [
        rcopy(kvsend.at[b], kvrows(CHAIN + PIECE * i), s_far.at[n], r_chain.at[i], dev(4 * b + e, y, x, c))
        for n, (b, e, i) in enumerate(far)
    ]
    for n in (2, 0, 1):
        far[n].start()
    for h in range(HEADS):
        qsend[h] = q_ref[:, h * HEAD : h * HEAD + HEAD]
    my_rows = qbuf.at[:, pl.ds(pl.multiple_of(128 * y, 128), 128), :]
    qs = [
        rcopy(qsend, my_rows, s_q.at[d - 1], r_q.at[d - 1], dev(z, (y + d) % 4, x, c)) for d in (1, 2, 3)
    ]
    for cp in qs:
        cp.start()
    own = [
        rcopy(
            kvsend.at[qz], kvrows(OWN + PIECE * zq), s_own.at[d - 1], r_own.at[d - 1],
            dev(4 * qz + (zq + d) % 4, y, x, c),
        )
        for d in (1, 2, 3)
    ]
    for cp in own:
        cp.start()
    near = [
        rcopy(
            skv_ref, kvrows(NEAR + 128 * zq, 128), s_near.at[d - 1], r_near.at[d - 1],
            dev(4 * qz + (zq + d) % 4, y, x, c),
        )
        for d in (1, 2, 3)
    ]
    for d in (1, 2, 3):
        pl.when(zq + d < 4)(near[d - 1].start)
    w0 = []
    for t in range(2):
        for k in range(2):
            yy = c + 2 * t
            cp = rcopy(w_ref, wbuf.at[ctx], s_w0.at[2 * t + k], r_w0.at[y], dev(z, yy, x, k))
            w0.append((cp, jnp.logical_not(jnp.logical_and(yy == y, k == c))))

    def w0_send():
        for cp, notself in w0:
            pl.when(notself)(cp.start)

    qbuf[:, pl.ds(pl.multiple_of(128 * y, 128), 128), :] = qsend[...]
    kv[:, pl.ds(pl.multiple_of(OWN + PIECE * zq, 32), PIECE), :] = kvsend[qz]
    for k in range(4):
        @pl.when(k == zq)
        def _():
            kv[:, 128 * k : 128 * k + 128, :] = skv_ref[...]

        @pl.when(k > zq)
        def _():
            kv[:, 128 * k : 128 * k + 128, :] = jnp.zeros((2, 128, HEAD), BF16)

    @pl.when(same)
    def _():
        wbuf[ctx] = w_ref[...]

    mst[...] = jnp.full(mst.shape, -1e30, F32)
    lst[...] = jnp.zeros(lst.shape, F32)
    acc[...] = jnp.zeros(acc.shape, F32)

    def link(idx, to):
        rows = kvrows(CHAIN + PIECE * idx)
        return rcopy(rows, rows, s_chain.at[idx // 6], r_chain.at[idx], dev(to, y, x, c))

    def chain(slot):
        for i, base, ok, to in (
            (slot - LAG * zq, 0, zq < 3, z + 1), (slot - LAG * (3 - zq), 6, zq > 0, z - 1)
        ):
            @pl.when(jnp.logical_and(i >= 0, i < 6))
            def _():
                cp = link(base + i, to)
                cp.wait_recv()
                pl.when(ok)(cp.start)

    def chain_sent():
        for n, ok in enumerate((zq < 3, zq > 0)):
            every = kvrows(CHAIN, 6 * PIECE)
            pl.when(ok)(rcopy(every, every, s_chain.at[n], r_chain.at[0], me).wait_send)

    sib = dev(z, y, x, 1 - c)

    def wpart(origin, j, cc):
        per = PARTS // 2
        rows = 64 // per
        first = pl.multiple_of(rows * (j % per), rows)
        return wbuf.at[4 * ((origin + 32) % 16) + 2 * cc + j // per, pl.ds(first, rows)]

    def wsend(e, way):
        t, j = e // PARTS, e % PARTS
        part = wpart(z - t if way else z + t, j, c)
        ssem, rsem = (s_w.at[0], r_wp) if way else (s_w.at[1], r_wm)
        return rcopy(part, part, ssem, rsem.at[e], dev((z + (1 if way else 15)) % 16, y, x, c))

    def wshare(t, way):
        block = wbuf.at[pl.ds(4 * (((z - t if way else z + t) + 32) % 16) + 2 * c, 2)]
        return rcopy(block, block, s_w.at[2], r_ws.at[0], sib)

    def wstart():
        def one(e, _):
            wsend(e, True).start()
            wsend(e, False).start()
            return 0

        lax.fori_loop(0, PARTS, one, 0)

    def wevents(first, last):
        def one(e, _):
            wsend(e, True).wait_recv()
            pl.when(e < 7 * PARTS)(wsend(e + PARTS, True).start)

            @pl.when(e < 7 * PARTS)
            def _():
                wsend(e, False).wait_recv()
                pl.when(e < 6 * PARTS)(wsend(e + PARTS, False).start)

            @pl.when(e % PARTS == PARTS - 1)
            def _():
                wshare(e // PARTS + 1, True).start()
                pl.when(e < 7 * PARTS)(wshare(e // PARTS + 1, False).start)

            return 0

        lax.fori_loop(first, last, one, 0)

    def wfinish():
        every = wbuf.at[pl.ds(0, 30)]
        rcopy(every, every, s_w.at[2], r_ws.at[0], sib).wait_recv()

    def wsent():
        for n, count in enumerate((16, 14, 30)):
            every = wbuf.at[pl.ds(0, count)]
            rcopy(every, every, s_w.at[n], r_ws.at[0], sib).wait_send()

    def attend(first, count, masked=False):
        rows = pl.ds(first if isinstance(first, int) else pl.multiple_of(first, 32), count)
        q = qbuf[...].reshape(HEADS * 512, HEAD)
        s = lax.dot_general(kv[0, rows], q, (((1,), (1,)), ((), ())), preferred_element_type=F32)
        if masked:
            key = lax.broadcasted_iota(jnp.int32, s.shape, 0)
            row = lax.broadcasted_iota(jnp.int32, s.shape, 1) % 512
            pos = (key // 128) * 512 + y * 128 + key % 128
            s = jnp.where(pos <= row + 512 * zq, s, -jnp.inf)
        before = mst[...]
        top = jnp.maximum(before, jnp.max(s, axis=0, keepdims=True))
        p = jnp.exp2((s - top) * SCALE_LOG2)
        shrink = jnp.exp2((before - top) * SCALE_LOG2)
        mst[...] = top
        lst[...] = lst[...] * shrink + jnp.sum(p, axis=0, keepdims=True)
        acc[...] = acc[...] * shrink + lax.dot_general(
            kv[1, rows], p.astype(BF16), (((0,), (0,)), ((), ())), preferred_element_type=F32
        )

    half = 3 * PIECE
    at = 0
    one_way = CHAIN + 6 * PIECE * (zq // 2)
    other_way = CHAIN + 6 * PIECE * (1 - zq // 2)
    def w0_wait(first):
        for k in range(2):
            yy = first + k
            cp = rcopy(w_ref, wbuf.at[4 * z + yy], s_w0.at[0], r_w0.at[yy], me)
            pl.when(jnp.logical_not(jnp.logical_and(same, yy == y)))(cp.wait_recv)

    def got_queries():
        for cp in qs:
            cp.wait_recv()

    def got_own():
        for cp in own:
            cp.wait_recv()

    def got_near():
        for d in (1, 2, 3):
            pl.when(zq >= d)(near[d - 1].wait_recv)

    def ring_begin():
        w0_wait(2 * c)
        wstart()

    work = {
        "w": w0_send, "q": got_queries, "o": got_own, "n": got_near, "r": ring_begin,
        "O": lambda: attend(OWN, 4 * PIECE),
        "N": lambda: attend(NEAR, 512, True),
        "A": lambda: attend(one_way, half),
        "B": lambda: attend(other_way, half),
        "C": lambda: attend(one_way + half, half),
        "D": lambda: attend(other_way + half, half),
    }
    for slot, (events, todo) in enumerate(SLOTS):
        if slot < 6 + 3 * LAG:
            chain(slot)
        for name in todo.split():
            work[name]()
        wevents(at, at + events)
        at += events

    ocp, scp = [], []
    for r in range(4):
        for h in range(HEADS):
            cols = slice(512 * h + 128 * r, 512 * h + 128 * r + 128)
            ost[r, h] = mst[:, cols]
            ost[r, HEADS + h] = lst[:, cols]
    for d in (2, 1, 3):
        r = (y + d) % 4
        scp.append(rcopy(ost.at[r], ostr.at[d - 1], s_st.at[d - 1], r_st.at[d - 1], dev(z, r, x, c)))
        scp[-1].start()
    for k in range(2):
        for h in (2 * k, 2 * k + 1):
            cols = slice(512 * h, 512 * h + 512)
            o = acc[:, cols] * (1.0 / lst[:, cols])
            for r in range(4):
                obuf[k, r, h % 2] = o[:, r * 128 : r * 128 + 128].astype(BF16)
        for d in (2, 1, 3):
            r, n = (y + d) % 4, 3 * k + d - 1
            ocp.append(rcopy(obuf.at[k, r], orecv.at[k, d - 1], s_o.at[n], r_o.at[n], dev(z, r, x, c)))
            ocp[-1].start()
        wevents(at, at + MID[k])
        at += MID[k]

    for k in range(2):
        for cp in (scp if k == 0 else []) + ocp[3 * k : 3 * k + 3]:
            cp.wait_recv()
        for h in range(2):
            ms = [ost[y, 2 * k + h]] + [ostr[n, 2 * k + h] for n in range(3)]
            ls = [ost[y, HEADS + 2 * k + h]] + [ostr[n, HEADS + 2 * k + h] for n in range(3)]
            os_ = [obuf[k, y, h]] + [orecv[k, n, h] for n in range(3)]
            top = jnp.maximum(jnp.maximum(ms[0], ms[1]), jnp.maximum(ms[2], ms[3]))
            ws = [l * jnp.exp2((m - top) * SCALE_LOG2) for m, l in zip(ms, ls)]
            inv = 1.0 / (ws[0] + ws[1] + ws[2] + ws[3])
            o = sum(o_.astype(F32) * (w * inv) for o_, w in zip(os_, ws))
            o = o.T.astype(BF16)
            abuf_out[k, :, h * HEAD : h * HEAD + HEAD] = o
            att_ref[:, (2 * k + h) * HEAD : (2 * k + h + 1) * HEAD] = o
        for d in (2, 1, 3, 0):
            for t in range(2):
                to = dev(z, ypair if t == 0 else y, (x + d) % 4, py)
                cp = rcopy(abuf_out.at[k], abuf.at[tp, k], s_a.at[0], r_a.at[0], to)
                if d == 0 and t == 1:
                    pl.when(jnp.logical_not(same))(cp.start)
                else:
                    cp.start()

        @pl.when(same)
        def _():
            abuf[tp, k] = abuf_out[k]

        wevents(at, at + LATE[k])
        at += LATE[k]

    wevents(at, 8 * PARTS)
    w0_wait(2 * (1 - c))
    wfinish()
    def every_a(count):
        return rcopy(abuf.at[pl.ds(0, count)], abuf.at[pl.ds(0, count)], s_a.at[0], r_a.at[0], sib)

    pl.when(same)(every_a(7).wait_recv)
    pl.when(jnp.logical_not(same))(every_a(8).wait_recv)

    def project(g, total):
        for k in range(2):
            w = wbuf[pl.ds(8 * g + 4 * k, 4)].reshape(256, 512)
            total = total + jnp.dot(abuf[g, k], w, preferred_element_type=F32)
        return total

    res[...] = lax.fori_loop(0, 8, project, jnp.zeros((128, 512), F32)).astype(BF16)
    out = rcopy(res, resrecv, s_out.at[0], r_out.at[0], dev(z, ypair, x, 1 - c))

    @pl.when(same)
    def _():
        mix_ref[...] = res[...]

    @pl.when(jnp.logical_not(same))
    def _():
        out.start()
        out.wait()
        mix_ref[...] = resrecv[...]

    for cp in far + qs + own + scp + ocp:
        cp.wait_send()
    for d in (1, 2, 3):
        pl.when(zq + d < 4)(near[d - 1].wait_send)
    for cp, ns in w0:
        pl.when(ns)(cp.wait_send)
    chain_sent()
    pl.when(same)(every_a(7).wait_send)
    pl.when(jnp.logical_not(same))(every_a(8).wait_send)
    wsent()


def body(queries, stretch_key_value, cache_kv, chosen, out_weight):
    dma = lambda n: pltpu.SemaphoreType.DMA((n,))
    vmem = pl.BlockSpec(memory_space=pltpu.VMEM)
    return pl.pallas_call(
        kernel,
        out_shape=(jax.ShapeDtypeStruct((128, 512), BF16), jax.ShapeDtypeStruct((128, 512), BF16)),
        in_specs=[vmem, vmem, vmem, pl.BlockSpec(memory_space=pltpu.SMEM), vmem],
        out_specs=(vmem, vmem),
        scratch_shapes=[
            pltpu.VMEM((4, 2, PIECE, HEAD), BF16),
            pltpu.VMEM((2, 2048, HEAD), BF16),
            pltpu.VMEM((HEADS, 128, HEAD), BF16),
            pltpu.VMEM((HEADS, 512, HEAD), BF16),
            pltpu.VMEM((HEAD, HEADS * 512), F32),
            pltpu.VMEM((1, HEADS * 512), F32),
            pltpu.VMEM((1, HEADS * 512), F32),
            pltpu.VMEM((2, 4, 2, HEAD, 128), BF16),
            pltpu.VMEM((4, 2 * HEADS, 1, 128), F32),
            pltpu.VMEM((2, 3, 2, HEAD, 128), BF16),
            pltpu.VMEM((3, 2 * HEADS, 1, 128), F32),
            pltpu.VMEM((8, 2, 128, 256), BF16),
            pltpu.VMEM((2, 128, 256), BF16),
            pltpu.VMEM((64, 64, 512), BF16),
            pltpu.VMEM((128, 512), BF16),
            pltpu.VMEM((128, 512), BF16),
        ]
        + [dma(n) for n in (3, 3, 3, 2, 3, 6, 3, 1, 4, 3, 1)]
        + [dma(n) for n in (3, 3, 12, 3, 6, 3, 1, 4, 8 * PARTS, 7 * PARTS, 1, 1)],
        compiler_params=pltpu.CompilerParams(
            collective_id=0, has_side_effects=True, vmem_limit_bytes=56 * 2**20
        ),
        cost_estimate=pl.CostEstimate(flops=2 * 2**30, bytes_accessed=4 * 2**20, transcendentals=2**22),
    )(queries, stretch_key_value, cache_kv, chosen.transpose(2, 0, 1), out_weight)


def solution(mesh):
    in_specs = (
        P("ctx", "tp"),
        P(None, "ctx", "tp"),
        P(None, None, "ctx", "tp"),
        P(),
        P("ctx", "tp"),
    )
    out_specs = (P("ctx", "tp"), P("ctx", "tp"))
    return jax.shard_map(body, mesh=mesh, in_specs=in_specs, out_specs=out_specs, check_vma=False)
```

time: 190 us -> 79.5 us (0.42)
  Pallas kernels: 185 us -> 75.6 us
    pallas_call x1, Pallas kernels: 185 us -> 75.6 us  [body(): pl.pallas_call(kernel, out_shape=(jax.ShapeDtypeStruct((128, 512), BF16),...]
    unnamed x3 -> x2, local copies, waits for them, and re-layouts: 4.52 us -> 3.14 us
where the time goes in v2:
time: 79.5 us; the launch traced here: 79.3 us
  Pallas kernels  75.6 us (95%)
  local copies, waits for them, and re-layouts  3.14 us (4%)
    pallas_call x1, Pallas kernels, body(): pl.pallas_call(kernel, out_shape=(jax.ShapeDtypeStruct((128, 512), BF16),...  75.6 us
    unnamed x2, local copies, waits for them, and re-layouts  3.14 us

profile of v2, /device:TPU:1, one launch (start us, length us, event | category | flops | bytes accessed | tf_op | source)
XLA Modules:
  0.0 79.3 jit_solution(16628899373153318680)
XLA Ops:
  0.6 75.6 %shard_map.68 = (bf16[128,512]{1,0:T(8,128)(2,1)}, bf16[128,512]{1,0:T(8,128)(2,1)}) custom-call(bf16[128,512]{1,0:T(8,128)(2,1)} %q_ref.1, bf16[2,128,128]{2,1,0:T(8,128)(2,1)} %skv_ref.1, bf16[2,128,32,128]{3,2,1,0:T(8,128)(2,1)} %cache_ref.1, s32[3,4,8]{2,1,0:T(4,128)} %bitcast.1, bf16[64,512]{1,0:T(8,128)(2,1)} %w_ref.1), custom_call_target="tpu_custom_call" | custom-call | flops 2147483648 | bytes 4194304 | tf_op jit(solution)/shard_map/pallas_call | solution.py:399
  76.2 1.6 %copy.9 = bf16[128,512]{1,0:T(8,128)(2,1)} copy(bf16[128,512]{1,0:T(8,128)(2,1)} %get-tuple-element.4) | data formatting | bytes 262144
  77.8 1.6 %copy.10 = bf16[128,512]{1,0:T(8,128)(2,1)} copy(bf16[128,512]{1,0:T(8,128)(2,1)} %get-tuple-element.5) | data formatting | bytes 262144

commit v3 on v2

--- a/solution.py
+++ b/solution.py
@@ -393,10 +393,15 @@
     wsent()
 
 
+def hand_over(att_in, mix_in, att_out, mix_out):
+    att_out[...] = att_in[...]
+    mix_out[...] = mix_in[...]
+
+
 def body(queries, stretch_key_value, cache_kv, chosen, out_weight):
     dma = lambda n: pltpu.SemaphoreType.DMA((n,))
     vmem = pl.BlockSpec(memory_space=pltpu.VMEM)
-    return pl.pallas_call(
+    results = pl.pallas_call(
         kernel,
         out_shape=(jax.ShapeDtypeStruct((128, 512), BF16), jax.ShapeDtypeStruct((128, 512), BF16)),
         in_specs=[vmem, vmem, vmem, pl.BlockSpec(memory_space=pltpu.SMEM), vmem],
@@ -426,6 +431,12 @@
         ),
         cost_estimate=pl.CostEstimate(flops=2 * 2**30, bytes_accessed=4 * 2**20, transcendentals=2**22),
     )(queries, stretch_key_value, cache_kv, chosen.transpose(2, 0, 1), out_weight)
+    return pl.pallas_call(
+        hand_over,
+        out_shape=tuple(jax.ShapeDtypeStruct(r.shape, r.dtype) for r in results),
+        in_specs=[vmem, vmem],
+        out_specs=(vmem, vmem),
+    )(*results)
 
 
 def solution(mesh):

time: 79.5 us -> 78.1 us (0.982)
  local copies, waits for them, and re-layouts: 3.14 us -> 0 us
  Pallas kernels: 75.6 us -> 77.2 us
    unnamed x2 -> x0, local copies, waits for them, and re-layouts: 3.14 us -> none
    pallas_call x0 -> x1, Pallas kernels: none -> 1.68 us  [body(): pl.pallas_call(hand_over, out_shape=tuple((jax.ShapeDtypeStruct(r.shape,...]
where the time goes in v3:
time: 78.1 us; the launch traced here: 77.9 us
  Pallas kernels  77.2 us (99%)
    pallas_call x1, Pallas kernels, body(): pl.pallas_call(kernel, out_shape=(jax.ShapeDtypeStruct((128, 512), BF16),...  75.6 us
    pallas_call x1, Pallas kernels, body(): pl.pallas_call(hand_over, out_shape=tuple((jax.ShapeDtypeStruct(r.shape,...  1.68 us

profile of v3, /device:TPU:1, one launch (start us, length us, event | category | flops | bytes accessed | tf_op | source)
XLA Modules:
  0.0 77.9 jit_solution(7069519650346915448)
XLA Ops:
  0.6 75.6 %shard_map.68 = (bf16[128,512]{1,0:T(8,128)(2,1)}, bf16[128,512]{1,0:T(8,128)(2,1)}) custom-call(bf16[128,512]{1,0:T(8,128)(2,1)} %q_ref.1, bf16[2,128,128]{2,1,0:T(8,128)(2,1)} %skv_ref.1, bf16[2,128,32,128]{3,2,1,0:T(8,128)(2,1)} %cache_ref.1, s32[3,4,8]{2,1,0:T(4,128)} %bitcast.1, bf16[64,512]{1,0:T(8,128)(2,1)} %w_ref.1), custom_call_target="tpu_custom_call" | custom-call | flops 2147483648 | bytes 4194304 | tf_op jit(solution)/shard_map/pallas_call | solution.py:404
  76.2 1.7 %shard_map.69 = (bf16[128,512]{1,0:T(8,128)(2,1)}, bf16[128,512]{1,0:T(8,128)(2,1)}) custom-call(bf16[128,512]{1,0:T(8,128)(2,1)} %get-tuple-element.4.att_in, bf16[128,512]{1,0:T(8,128)(2,1)} %get-tuple-element.5.mix_in), custom_call_target="tpu_custom_call" | custom-call | tf_op jit(solution)/shard_map/pallas_call | solution.py:434

commit v4 on v3

--- a/solution.py
+++ b/solution.py
@@ -21,8 +21,8 @@
 
 
 def kernel(
-    q_ref, skv_ref, cache_ref, chosen_ref, w_ref, att_ref, mix_ref,
-    kvsend, kv, qsend, qbuf, acc, mst, lst, obuf, ost, orecv, ostr, abuf, abuf_out, wbuf, res, resrecv,
+    q_ref, skv_ref, cache_hbm, chosen_ref, w_ref, att_ref, mix_ref,
+    cache_ref, cache_sem, kvsend, kv, qsend, qbuf, acc, mst, lst, obuf, ost, orecv, ostr, abuf, abuf_out, wbuf, res, resrecv,
     s_far, s_own, s_near, s_chain, s_q, s_o, s_st, s_a, s_w0, s_w, s_out,
     r_own, r_near, r_chain, r_q, r_o, r_st, r_a, r_w0, r_wp, r_wm, r_ws, r_out,
 ):
@@ -42,6 +42,9 @@
         )
 
     me = dev(z, y, x, c)
+
+    fetch = pltpu.make_async_copy(cache_hbm, cache_ref, cache_sem)
+    fetch.start()
 
     barrier = pltpu.get_barrier_semaphore()
 
@@ -86,7 +89,14 @@
                     greet(dev(z, mine, xx, k))
             else:
                 greet(dev(z, mine, xx, k))
+    mst[...] = jnp.full(mst.shape, -1e30, F32)
+    lst[...] = jnp.zeros(lst.shape, F32)
+    acc[...] = jnp.zeros(acc.shape, F32)
+    for h in range(HEADS):
+        qsend[h] = q_ref[:, h * HEAD : h * HEAD + HEAD]
     pl.semaphore_wait(barrier, 24 - 2 * same.astype(jnp.int32))
+
+    fetch.wait()
 
     for b in range(4):
         for j in range(3):
@@ -109,8 +119,6 @@
     ]
     for n in (2, 0, 1):
         far[n].start()
-    for h in range(HEADS):
-        qsend[h] = q_ref[:, h * HEAD : h * HEAD + HEAD]
     my_rows = qbuf.at[:, pl.ds(pl.multiple_of(128 * y, 128), 128), :]
     qs = [
         rcopy(qsend, my_rows, s_q.at[d - 1], r_q.at[d - 1], dev(z, (y + d) % 4, x, c)) for d in (1, 2, 3)
@@ -161,9 +169,6 @@
     def _():
         wbuf[ctx] = w_ref[...]
 
-    mst[...] = jnp.full(mst.shape, -1e30, F32)
-    lst[...] = jnp.zeros(lst.shape, F32)
-    acc[...] = jnp.zeros(acc.shape, F32)
 
     def link(idx, to):
         rows = kvrows(CHAIN + PIECE * idx)
@@ -404,9 +409,13 @@
     results = pl.pallas_call(
         kernel,
         out_shape=(jax.ShapeDtypeStruct((128, 512), BF16), jax.ShapeDtypeStruct((128, 512), BF16)),
-        in_specs=[vmem, vmem, vmem, pl.BlockSpec(memory_space=pltpu.SMEM), vmem],
+        in_specs=[
+            vmem, vmem, pl.BlockSpec(memory_space=pl.ANY), pl.BlockSpec(memory_space=pltpu.SMEM), vmem
+        ],
         out_specs=(vmem, vmem),
         scratch_shapes=[
+            pltpu.VMEM((2, 128, 32, HEAD), BF16),
+            pltpu.SemaphoreType.DMA,
             pltpu.VMEM((4, 2, PIECE, HEAD), BF16),
             pltpu.VMEM((2, 2048, HEAD), BF16),
             pltpu.VMEM((HEADS, 128, HEAD), BF16),

time: 78.1 us -> 77.3 us (0.990)
  no operation moved by 1% of the time
where the time goes in v4:
time: 77.3 us; the launch traced here: 77.1 us
  Pallas kernels  76.5 us (99%)
    pallas_call x1, Pallas kernels, body(): pl.pallas_call(kernel, out_shape=(jax.ShapeDtypeStruct((128, 512), BF16),...  74.8 us
    pallas_call x1, Pallas kernels, body(): pl.pallas_call(hand_over, out_shape=tuple((jax.ShapeDtypeStruct(r.shape,...  1.68 us

profile of v4, /device:TPU:1, one launch (start us, length us, event | category | flops | bytes accessed | tf_op | source)
XLA Modules:
  0.0 77.1 jit_solution(5030339455518127996)
XLA Ops:
  0.6 74.8 %shard_map.68 = (bf16[128,512]{1,0:T(8,128)(2,1)}, bf16[128,512]{1,0:T(8,128)(2,1)}) custom-call(bf16[128,512]{1,0:T(8,128)(2,1)} %q_ref.1, bf16[2,128,128]{2,1,0:T(8,128)(2,1)} %skv_ref.1, bf16[2,128,32,128]{3,2,1,0:T(8,128)(2,1)} %cache_hbm.1, s32[3,4,8]{2,1,0:T(4,128)} %bitcast.1, bf16[64,512]{1,0:T(8,128)(2,1)} %w_ref.1), custom_call_target="tpu_custom_call" | custom-call | flops 2147483648 | bytes 4194304 | tf_op jit(solution)/shard_map/pallas_call | solution.py:409
  75.5 1.7 %shard_map.69 = (bf16[128,512]{1,0:T(8,128)(2,1)}, bf16[128,512]{1,0:T(8,128)(2,1)}) custom-call(bf16[128,512]{1,0:T(8,128)(2,1)} %get-tuple-element.4.att_in, bf16[128,512]{1,0:T(8,128)(2,1)} %get-tuple-element.5.mix_in), custom_call_target="tpu_custom_call" | custom-call | tf_op jit(solution)/shard_map/pallas_call | solution.py:443
